TPU v7x, 32 devices: a whole 2x2x4 slice. The times are simulated.
32 devices in a mesh: tm: 16 (over z, y, core), plane: 2 (over x).
Axes of the slice: x: 2, y: 2, z: 4, core: 2. Of those that a mesh axis runs over, the one named last changes fastest.
Arguments:
- frames: bfloat16 [16, 4, 128, 256], P('tm', 'plane'), may hold values from -6 to 6
- offsets: int32 [16, 4, 2], P('tm', 'plane'), may hold values from -64 to 64
- assign: int32 [16, 4, 1, 2, 1], P('tm', 'plane'), may hold values from 0 to 1; in each aligned block of 4 rows (0 to 3, 4 to 7, ..., all dimensions but the last counted through in order) at most 4 rows name the same one
- residual: int32 [16, 4, 1, 2, 2], P('tm', 'plane'), may hold values from -8 to 8
- template: bfloat16 [4, 128, 256], P(None, None, 'plane'), may hold values from -6 to 6
Outputs:
- new_template: bfloat16 [4, 128, 256], P(None, None, 'plane')
- scores: float32 [2, 16, 4, 1, 2], P(None, 'tm', 'plane')
Inputs may be any that keep to these rules, and one draw needn't show every extreme that they name: `assign`: in each aligned block of 4 rows (the patches of one volume and one plane group), no column is named more than 4 times; one column is named exactly 4 times in some block.
All inputs are finite; a program needn't handle non-finite values.
Results may differ from a plain program's by a relative error of at most 0.004.
Values may be sent and summed in bfloat16 or wider, within the bound.
A program may use at most 64 MiB of HBM per device.

v0:
```python
import math

import jax
import jax.numpy as jnp
from jax import lax
from jax.sharding import PartitionSpec as P

ROUNDS = 2


highest = lax.Precision.HIGHEST


def dft_tables(length):
    indices = jnp.arange(length, dtype=jnp.int32)
    phases = (indices[:, None] * indices[None, :] % length).astype(jnp.float32) * (
        2.0 * math.pi / length
    )
    return (jnp.cos(phases).astype(jnp.bfloat16), jnp.sin(phases).astype(jnp.bfloat16))


def cyclic(source, amount, which_axis):
    length = source.shape[which_axis]
    doubled = jnp.concatenate([source, source], which_axis)
    return lax.dynamic_slice_in_dim(
        doubled, (amount % length).astype(jnp.int32), length, which_axis
    )


def shift_plane(frame_img, plane_off):
    return cyclic(cyclic(frame_img, plane_off[0], 0), plane_off[1], 1)


def to_tiles(tile_batch, patch_size):
    plane_count, tall, broad = tile_batch.shape
    shaped = tile_batch.reshape(
        plane_count, tall // patch_size, patch_size, broad // patch_size, patch_size
    )
    return shaped.transpose(0, 1, 3, 2, 4)


def spectrum(tile_batch, cos_t, sin_t):
    first_re = jnp.einsum(
        "nyx,xk->nyk", tile_batch, cos_t, preferred_element_type=jnp.float32
    ).astype(jnp.bfloat16)
    first_im = (
        -jnp.einsum("nyx,xk->nyk", tile_batch, sin_t, preferred_element_type=jnp.float32)
    ).astype(jnp.bfloat16)
    spec_re = jnp.einsum(
        "uy,nyk->nuk", cos_t, first_re, preferred_element_type=jnp.float32
    ) + jnp.einsum("uy,nyk->nuk", sin_t, first_im, preferred_element_type=jnp.float32)
    spec_im = jnp.einsum(
        "uy,nyk->nuk", cos_t, first_im, preferred_element_type=jnp.float32
    ) - jnp.einsum("uy,nyk->nuk", sin_t, first_re, preferred_element_type=jnp.float32)
    return (spec_re, spec_im)


def assess(patches, temp_re, temp_im, shift_rows, shift_cols, live_mask, cos_t, sin_t):
    patch_size = patches.shape[1]
    patch_re, patch_im = spectrum(patches, cos_t, sin_t)
    cross_re = patch_re * temp_re + patch_im * temp_im
    cross_im = patch_im * temp_re - patch_re * temp_im
    modulus = jnp.sqrt(cross_re * cross_re + cross_im * cross_im)
    levels = jnp.mean(modulus, axis=(1, 2), keepdims=True)
    divisor = modulus + 0.1 * levels + 1e-06
    norm_re = (cross_re / divisor).astype(jnp.bfloat16)
    norm_im = (cross_im / divisor).astype(jnp.bfloat16)
    row_a = (shift_rows % patch_size).astype(jnp.int32)
    row_b = (shift_cols % patch_size).astype(jnp.int32)
    cos_a = cos_t[row_a].astype(jnp.float32)
    sin_a = sin_t[row_a].astype(jnp.float32)
    cos_b = cos_t[row_b]
    sin_b = sin_t[row_b]
    re_cos = jnp.einsum("nuv,nv->nu", norm_re, cos_b, preferred_element_type=jnp.float32)
    re_sin = jnp.einsum("nuv,nv->nu", norm_re, sin_b, preferred_element_type=jnp.float32)
    im_cos = jnp.einsum("nuv,nv->nu", norm_im, cos_b, preferred_element_type=jnp.float32)
    im_sin = jnp.einsum("nuv,nv->nu", norm_im, sin_b, preferred_element_type=jnp.float32)
    scores = (
        jnp.sum(cos_a * re_cos, 1)
        - jnp.sum(sin_a * re_sin, 1)
        - jnp.sum(sin_a * im_cos, 1)
        - jnp.sum(cos_a * im_sin, 1)
    ) / patch_size
    weights = (0.5 + jax.nn.sigmoid(scores)) * live_mask
    registered = jax.vmap(
        lambda single, shift_down, shift_across: cyclic(
            cyclic(single, shift_down, 0), shift_across, 1
        )
    )(patches, shift_rows, shift_cols)
    contrib = registered.astype(jnp.float32) * weights[:, None, None]
    return (contrib, weights, scores)


def renew(old_rows_all, tile_sums, weight_sums, patch_size):
    totals, weight_all = lax.psum((tile_sums, weight_sums), "tm")
    return (
        (old_rows_all.astype(jnp.float32) + totals)
        / (1.0 + jnp.repeat(weight_all, patch_size))[:, None]
    ).astype(jnp.bfloat16)


def local(frames, offsets, assign, residual, template):
    patch_size = template.shape[2]
    planes_all = template.shape[0]
    grid_rows = template.shape[1] // patch_size
    owners = lax.axis_size("plane")
    plane_dev = frames.shape[1]
    patch_count = plane_dev * grid_rows * owners
    capacity = 2 * patch_count // owners
    plane_group = lax.axis_index("plane")
    cos_t, sin_t = dft_tables(patch_size)
    shifted = jax.vmap(shift_plane)(frames[0], offsets[0])
    patches = to_tiles(shifted, patch_size).reshape(patch_count, patch_size, patch_size)
    owner_col = assign.reshape(patch_count)
    shift_rows = residual[0, :, :, :, 0].reshape(patch_count)
    shift_cols = residual[0, :, :, :, 1].reshape(patch_count)
    counter = jnp.arange(patch_count, dtype=jnp.int32)
    plane_local = counter // (grid_rows * owners)
    row_local = counter // owners % grid_rows
    score_list = []
    column_hit = (owner_col[:, None] == jnp.arange(owners, dtype=jnp.int32)[None, :]).astype(
        jnp.int32
    )
    position = jnp.sum(jnp.cumsum(column_hit, 0) * column_hit, 1) - 1
    slot_index = owner_col * capacity + position
    slot_count = owners * capacity
    placing = slot_index[:, None] == jnp.arange(slot_count, dtype=jnp.int32)[None, :]
    outgoing = jnp.einsum(
        "rs,rxy->sxy", placing.astype(jnp.bfloat16), patches, preferred_element_type=jnp.float32
    ).astype(jnp.bfloat16)
    outgoing = outgoing.reshape(owners, capacity, patch_size, patch_size)
    details = jnp.stack(
        [
            plane_group * plane_dev + plane_local,
            row_local,
            shift_rows,
            shift_cols,
            jnp.ones_like(shift_rows),
        ],
        1,
    )
    outgoing_info = jnp.sum(placing.astype(jnp.int32)[:, :, None] * details[:, None, :], 0).reshape(
        owners, capacity, 5
    )
    current = template
    for round_index in range(ROUNDS):
        tile_stack = current
        temp_re, temp_im = spectrum(tile_stack, cos_t, sin_t)
        arrived = lax.all_to_all(outgoing, "plane", split_axis=0, concat_axis=0, tiled=True)
        arrived_info = lax.all_to_all(
            outgoing_info, "plane", split_axis=0, concat_axis=0, tiled=True
        )
        senders = arrived.shape[0]
        held_slots = arrived.shape[1]
        flat_info = arrived_info.reshape(senders * held_slots, 5)
        target = flat_info[:, 0] * grid_rows + flat_info[:, 1]
        contrib, weights, scores = assess(
            arrived.reshape(senders * held_slots, patch_size, patch_size),
            temp_re[target],
            temp_im[target],
            flat_info[:, 2],
            flat_info[:, 3],
            flat_info[:, 4].astype(jnp.float32),
            cos_t,
            sin_t,
        )
        contrib, weights, scores, target = (
            contrib.reshape(senders, held_slots, patch_size, patch_size),
            weights.reshape(senders, held_slots),
            scores.reshape(senders, held_slots),
            target.reshape(senders, held_slots),
        )
        returned = lax.all_to_all(scores, "plane", split_axis=0, concat_axis=0, tiled=True)
        score_rows = jnp.sum(placing.astype(jnp.float32) * returned.reshape(1, slot_count), 1)
        score_list.append(score_rows.reshape(plane_dev, grid_rows, owners))
        onehot = (
            target.reshape(slot_count)[:, None]
            == jnp.arange(planes_all * grid_rows, dtype=jnp.int32)[None, :]
        ).astype(jnp.float32)
        tile_sums = jnp.einsum(
            "st,sxy->txy",
            onehot,
            contrib.reshape(slot_count, patch_size, patch_size),
            precision=highest,
        )
        weight_sums = jnp.dot(weights.reshape(slot_count), onehot, precision=highest)
        renewed = renew(
            current.reshape(planes_all * grid_rows * patch_size, patch_size),
            tile_sums.reshape(planes_all * grid_rows * patch_size, patch_size),
            weight_sums,
            patch_size,
        )
        current = renewed.reshape(planes_all, grid_rows * patch_size, patch_size)
    return (current, jnp.stack(score_list)[:, None])


def solution(mesh):
    return jax.shard_map(
        local,
        mesh=mesh,
        in_specs=(
            P("tm", "plane", None, None),
            P("tm", "plane", None),
            P("tm", "plane", None, None, None),
            P("tm", "plane", None, None, None),
            P(None, None, "plane"),
        ),
        out_specs=(P(None, None, "plane"), P(None, "tm", "plane", None, None)),
        check_vma=False,
    )
```

profile of v0, /device:TPU:0, one launch (start us, length us, event | category | flops | bytes accessed | tf_op | source)
XLA Modules:
  0.0 239.3 jit_solution(16732155745536902916)
XLA Ops:
  7.8 0.7 reduce.31
  8.8 0.7 copy-done.2
  10.1 0.7 copy.68
  10.7 4.2 %all-to-all-start = ((s32[2,4,5]{2,1,0:T(4,128)}), s32[2,4,5]{2,1,0:T(4,128)S(1)}, u32[]{:S(2)}, u32[]{:S(2)}) async-start(s32[2,4,5]{2,1,0:T(4,128)} %bitcast.1), calls=%async_computation | async-start | bytes 8192 | tf_op jit(solution)/shard_map/all_to_all | solution.py:150
  15.0 1.4 fusion.10
  17.9 0.7 copy-done.3
  18.8 0.9 gather_fusion.8
  20.3 0.9 gather_fusion.9
  23.4 0.8 copy.72
  24.2 3.4 %all-to-all-start.1 = ((bf16[2,4,128,128]{3,1,2,0:T(4,128)(2,1)}), bf16[2,4,128,128]{3,1,2,0:T(4,128)(2,1)S(1)}, u32[]{:S(2)}, u32[]{:S(2)}) async-start(bf16[2,4,128,128]{3,1,2,0:T(4,128)(2,1)} %copy.72), calls=%async_computation.1 | async-start | bytes 524288 | tf_op jit(solution)/shard_map/all_to_all | solution.py:149
  31.0 0.6 gather_fusion.1
  31.8 1.5 all-to-all-done.1
  35.8 0.8 fusion.11
  38.0 1.3 gather_fusion.10
  39.9 1.3 gather_fusion.11
  42.5 0.7 copy.81
  43.2 32.9 %psum.29 = f32[4]{0:T(128)S(1)} all-reduce(f32[4]{0:T(128)S(1)} %convolution_bitcast_fusion.1), channel_id=1, replica_groups=mesh['tm'=16,'plane'=2] {'tm'}, use_global_device_ids=true, to_apply=%region_9.10 | all-reduce | flops 4 | bytes 32 | tf_op jit(solution)/shard_map/psum | solution.py:95
  76.1 0.6 div.75
  76.8 3.2 %all-to-all-start.2 = ((f32[2,1,4]{2,1,0:T(1,128)}), f32[2,1,4]{2,1,0:T(1,128)S(1)}, u32[]{:S(2)}, u32[]{:S(2)}) async-start(f32[2,1,4]{2,1,0:T(1,128)} %bitcast.50), calls=%async_computation.2 | async-start | bytes 2048 | tf_op jit(solution)/shard_map/all_to_all | solution.py:173
  80.1 3.5 %all-to-all-done.2 = f32[2,1,4]{2,1,0:T(1,128)S(1)} async-done(((f32[2,1,4]{2,1,0:T(1,128)}), f32[2,1,4]{2,1,0:T(1,128)S(1)}, u32[]{:S(2)}, u32[]{:S(2)}) %all-to-all-start.2) | async-done | bytes 64 | tf_op jit(solution)/shard_map/all_to_all | solution.py:173
  84.1 0.7 reduce.33
  84.9 48.0 %all-reduce.7.cloned.1.call-done = f32[512,128]{1,0:T(8,128)} async-done(((f32[512,128]{1,0:T(8,128)}), f32[512,128]{1,0:T(8,128)}) %all-reduce.7.cloned.1.call-update) | async-done | bytes 262160 | tf_op jit(solution)/shard_map/psum | solution.py:95
  132.9 1.1 fusion.14
  136.1 0.6 gather_fusion.7
  137.2 0.6 gather_fusion.6
  140.5 0.7 copy.87
  141.2 32.0 %psum.31 = f32[4]{0:T(128)S(1)} all-reduce(f32[4]{0:T(128)S(1)} %convolution_bitcast_fusion), channel_id=1, replica_groups=mesh['tm'=16,'plane'=2] {'tm'}, use_global_device_ids=true, to_apply=%region_16.17 | all-reduce | flops 4 | bytes 32 | tf_op jit(solution)/shard_map/psum | solution.py:95
  173.4 6.2 %all_to_all.24 = f32[2,1,4]{2,1,0:T(1,128)S(1)} all-to-all(f32[2,1,4]{2,1,0:T(1,128)S(1)} %bitcast.181), channel_id=1, replica_groups=mesh['tm'=16,'plane'=2] {'plane'}, dimensions={0} | all-to-all | bytes 64 | tf_op jit(solution)/shard_map/all_to_all | solution.py:173
  179.6 0.7 reduce.32
  180.7 0.6 pad_maximum_fusion.4
  181.3 49.4 %all-reduce.9.cloned.1.call-done = f32[512,128]{1,0:T(8,128)} async-done(((f32[512,128]{1,0:T(8,128)}), f32[512,128]{1,0:T(8,128)}) %all-reduce.9.cloned.1.call-update) | async-done | bytes 262160 | tf_op jit(solution)/shard_map/psum | solution.py:95
  230.7 1.7 divide_convert_fusion.4
  (105 shorter events, 21.6 us)
Async XLA Ops:
  7.2 0.7 copy-start.4
  8.8 0.7 copy-start.2
  10.7 13.4 %all-to-all-start = ((s32[2,4,5]{2,1,0:T(4,128)}), s32[2,4,5]{2,1,0:T(4,128)S(1)}, u32[]{:S(2)}, u32[]{:S(2)}) async-start(s32[2,4,5]{2,1,0:T(4,128)} %bitcast.1), calls=%async_computation | async-start | bytes 8192 | tf_op jit(solution)/shard_map/all_to_all | solution.py:150
  15.0 1.4 copy-start.1
  16.4 1.0 copy-start
  17.9 0.7 copy-start.3
  24.2 9.1 %all-to-all-start.1 = ((bf16[2,4,128,128]{3,1,2,0:T(4,128)(2,1)}), bf16[2,4,128,128]{3,1,2,0:T(4,128)(2,1)S(1)}, u32[]{:S(2)}, u32[]{:S(2)}) async-start(bf16[2,4,128,128]{3,1,2,0:T(4,128)(2,1)} %copy.72), calls=%async_computation.1 | async-start | bytes 524288 | tf_op jit(solution)/shard_map/all_to_all | solution.py:149
  27.6 105.3 %all-reduce.7.cloned.1.call-start = ((), (), s32[]{:S(2)}) async-start(), calls=%async_computation.4 | async-start | bytes 524288 | tf_op jit(solution)/shard_map/psum | solution.py:95
  76.8 6.9 %all-to-all-start.2 = ((f32[2,1,4]{2,1,0:T(1,128)}), f32[2,1,4]{2,1,0:T(1,128)S(1)}, u32[]{:S(2)}, u32[]{:S(2)}) async-start(f32[2,1,4]{2,1,0:T(1,128)} %bitcast.50), calls=%async_computation.2 | async-start | bytes 2048 | tf_op jit(solution)/shard_map/all_to_all | solution.py:173
  80.0 150.8 %all-reduce.9.cloned.1.call-start = ((), (), s32[]{:S(2)}) async-start(), calls=%async_computation.5 | async-start | bytes 524288 | tf_op jit(solution)/shard_map/psum | solution.py:95
Sparse Core Ops, SparseCore 0:
  43.4 89.5 all-reduce.6
  141.3 89.3 all-reduce.8
where the time goes:
time: 240 us; the launch traced here: 239 us
  waiting for transfers between devices  103 us (43%)
  blocking collectives  71.1 us (30%)
  local copies, waits for them, and re-layouts  18.3 us (8%)
  between operations  14.5 us (6%)
  matrix products  11.9 us (5%)
  starting transfers between devices  11.1 us (5%)
  other arithmetic  9.81 us (4%)
    psum x2, waiting for transfers between devices, renew(): totals, weight_all = lax.psum((tile_sums, weight_sums), 'tm')  97.5 us
    psum x2, blocking collectives, renew(): totals, weight_all = lax.psum((tile_sums, weight_sums), 'tm')  64.9 us
    all_to_all x1, blocking collectives, local(): lax.all_to_all(scores, 'plane', split_axis=0, concat_axis=0, tiled=True)  6.25 us
  transfers between devices with their start and end apart: 5, of which 4 were waited for; matrix products, arithmetic and copies ran while one was open for 7% of the time, Pallas kernels for 0%

commit v1 on v0

--- a/solution.py
+++ b/solution.py
@@ -1,8 +1,13 @@
+import functools
 import math
 
 import jax
 import jax.numpy as jnp
+import ml_dtypes
+import numpy as np
 from jax import lax
+from jax.experimental import pallas as pl
+from jax.experimental.pallas import tpu as pltpu
 from jax.sharding import PartitionSpec as P
 
 ROUNDS = 2
@@ -194,9 +199,332 @@
     return (current, jnp.stack(score_list)[:, None])
 
 
+CHUNK = 16
+MESH = pl.DeviceIdType.MESH
+
+
+def trig_table(length):
+    index = np.arange(length)
+    phases = (index[:, None] * index[None, :] % length) * (2.0 * np.pi / length)
+    return np.concatenate([np.cos(phases), np.sin(phases)], 1).astype(ml_dtypes.bfloat16)
+
+
+def mxu(left, right):
+    return jnp.dot(left, right, preferred_element_type=jnp.float32)
+
+
+def wrapped_eye(length, amount, axis):
+    near = lax.broadcasted_iota(jnp.int32, (length, length), axis)
+    far = lax.broadcasted_iota(jnp.int32, (length, length), 1 - axis)
+    return (((near + amount) & (length - 1)) == far).astype(jnp.float32).astype(jnp.bfloat16)
+
+
+def two_stage(tile, table):
+    size = tile.shape[0]
+    first = mxu(tile, table)
+    first_re = first[:, :size].astype(jnp.bfloat16)
+    neg_re = (-first[:, :size]).astype(jnp.bfloat16)
+    first_im = (-first[:, size:]).astype(jnp.bfloat16)
+    stacked = jnp.concatenate(
+        [
+            jnp.concatenate([first_re, first_im], 1),
+            jnp.concatenate([first_im, neg_re], 1),
+        ],
+        0,
+    )
+    return mxu(table, stacked)
+
+
+def fused_kernel(
+    n_tm, cols, plane_dev, info_ref, frames_ref, template_ref, table_ref, out_ref, scores_ref,
+    temp_a, temp_b, reg_src, reg_buf, w_src, w_buf, fin, spec,
+    swap_s, swap_r, reg_s, reg_r, w_s, w_r, t_s, t_r, f_s, f_r,
+):
+    size = table_ref.shape[0]
+    chunks = size // CHUNK
+    patch_count = plane_dev * cols
+    me = lax.axis_index("tm")
+    group = lax.axis_index("plane")
+    flat = me * cols + group
+    off_at, assign_at, res_at = 0, 2 * plane_dev, 2 * plane_dev + patch_count
+
+    def place(owner):
+        plane = owner // chunks
+        row = pl.multiple_of((owner % chunks) * CHUNK, CHUNK)
+        return plane, pl.ds(row, CHUNK)
+
+    my_plane, my_rows = place(me)
+
+    def around(body):
+        def step(r, carry):
+            body(lax.rem(me + r, n_tm))
+            return carry
+
+        lax.fori_loop(1, n_tm, step, 0)
+
+    def across(body):
+        def step(r, carry):
+            body(lax.rem(group + r, cols))
+            return carry
+
+        lax.fori_loop(1, cols, step, 0)
+
+    def everyone(body):
+        def step(r, carry):
+            other = lax.rem(flat + r, n_tm * cols)
+            body(other, other // cols, lax.rem(other, cols))
+            return carry
+
+        lax.fori_loop(1, n_tm * cols, step, 0)
+
+    barrier = pltpu.get_barrier_semaphore()
+    around(
+        lambda j: pl.semaphore_signal(barrier, inc=1, device_id=(j, group), device_id_type=MESH)
+    )
+    across(lambda h: pl.semaphore_signal(barrier, inc=1, device_id=(me, h), device_id_type=MESH))
+
+    table = table_ref[...]
+
+    patches = []
+    for plane in range(plane_dev):
+        frame = frames_ref[0, plane]
+        rows = mxu(wrapped_eye(size, info_ref[off_at + 2 * plane], 0), frame).astype(jnp.bfloat16)
+        shifted = mxu(
+            rows, wrapped_eye(frame.shape[1], info_ref[off_at + 2 * plane + 1], 1)
+        ).astype(jnp.bfloat16)
+        for col in range(cols):
+            patches.append(shifted[:, col * size : (col + 1) * size])
+    for q, patch in enumerate(patches):
+        rolled = mxu(wrapped_eye(size, info_ref[res_at + 2 * q], 0), patch).astype(jnp.bfloat16)
+        rolled = mxu(rolled, wrapped_eye(size, info_ref[res_at + 2 * q + 1], 1))
+        reg_src[q // cols, q % cols] = rolled.astype(jnp.bfloat16)
+
+    pl.semaphore_wait(barrier, n_tm - 1 + cols - 1)
+
+    def swap_copy(to, slot):
+        return pltpu.make_async_remote_copy(
+            src_ref=template_ref.at[pl.ds(to * plane_dev, plane_dev)],
+            dst_ref=temp_a.at[slot],
+            send_sem=swap_s.at[to],
+            recv_sem=swap_r.at[slot],
+            device_id=(me, to),
+            device_id_type=MESH,
+        )
+
+    def reg_copy(to, slot):
+        plane, rows = place(to)
+        return pltpu.make_async_remote_copy(
+            src_ref=reg_src.at[plane, :, rows, :],
+            dst_ref=reg_buf.at[slot],
+            send_sem=reg_s.at[to],
+            recv_sem=reg_r.at[slot],
+            device_id=(to, group),
+            device_id_type=MESH,
+        )
+
+    def w_copy(k, to, slot):
+        return pltpu.make_async_remote_copy(
+            src_ref=w_src.at[k, to // chunks],
+            dst_ref=w_buf.at[k, slot],
+            send_sem=w_s.at[k, to],
+            recv_sem=w_r.at[k, slot],
+            device_id=(to, group),
+            device_id_type=MESH,
+        )
+
+    def t_copy(to, owner):
+        plane, rows = place(owner)
+        return pltpu.make_async_remote_copy(
+            src_ref=temp_b.at[:, plane, rows, :],
+            dst_ref=temp_b.at[:, plane, rows, :],
+            send_sem=t_s.at[to],
+            recv_sem=t_r.at[owner],
+            device_id=(to, group),
+            device_id_type=MESH,
+        )
+
+    def f_copy(to, to_tm, to_plane, owner, owner_tm, owner_plane):
+        plane, rows = place(owner_tm)
+        return pltpu.make_async_remote_copy(
+            src_ref=fin.at[to_plane],
+            dst_ref=out_ref.at[owner_plane * plane_dev + plane, rows, :],
+            send_sem=f_s.at[to],
+            recv_sem=f_r.at[owner],
+            device_id=(to_tm, to_plane),
+            device_id_type=MESH,
+        )
+
+    across(lambda h: swap_copy(h, group).start())
+    around(lambda j: reg_copy(j, me).start())
+    temp_a[group] = template_ref[pl.ds(group * plane_dev, plane_dev)]
+    reg_buf[me] = reg_src[my_plane, :, my_rows, :]
+
+    for q, patch in enumerate(patches):
+        spec[q] = two_stage(patch, table)
+
+    row_id = lax.broadcasted_iota(jnp.int32, (2 * patch_count, size), 0)
+    lane_id = lax.broadcasted_iota(jnp.int32, (2 * patch_count, size), 1)
+    wanted = jnp.zeros((2 * patch_count, size), jnp.int32)
+    for q in range(patch_count):
+        wanted = jnp.where(row_id == q, info_ref[res_at + 2 * q], wanted)
+        wanted = jnp.where(row_id == patch_count + q, info_ref[res_at + 2 * q + 1], wanted)
+    onehot = ((wanted & (size - 1)) == lane_id).astype(jnp.float32).astype(jnp.bfloat16)
+    picked = mxu(onehot, table)
+    left = jnp.concatenate(
+        [picked[:patch_count, :size], picked[:patch_count, size:]], 0
+    ).astype(jnp.bfloat16)
+
+    block_row = lax.broadcasted_iota(jnp.int32, (8, size), 0)
+    across(lambda h: swap_copy(h, h).wait_recv())
+
+    score_rows = jnp.zeros((8, size), jnp.float32)
+    for k in range(ROUNDS):
+        temp = temp_a if k == 0 else temp_b
+        blocks = [jnp.zeros((8, size), jnp.float32) for _ in range(plane_dev)]
+        for q in range(patch_count):
+            plane, col = q // cols, q % cols
+            target = jnp.full((size, size), info_ref[assign_at + q], jnp.int32)
+            tile = temp[0, plane].astype(jnp.float32)
+            for c in range(1, cols):
+                tile = jnp.where(target == c, temp[c, plane].astype(jnp.float32), tile)
+            temp_spec = two_stage(tile.astype(jnp.bfloat16), table)
+            temp_re, temp_im = temp_spec[:, :size], temp_spec[:, size:]
+            patch_re, patch_im = spec[q, :, :size], spec[q, :, size:]
+            cross_re = patch_re * temp_re + patch_im * temp_im
+            cross_im = patch_im * temp_re - patch_re * temp_im
+            modulus = jnp.sqrt(cross_re * cross_re + cross_im * cross_im)
+            level = jnp.sum(modulus, axis=0, keepdims=True)
+            level = jnp.sum(level, axis=1, keepdims=True) * (1.0 / (size * size))
+            inverse = 1.0 / (modulus + (0.1 * level + 1e-06))
+            norm = jnp.concatenate(
+                [
+                    (cross_re * inverse).astype(jnp.bfloat16),
+                    (cross_im * inverse).astype(jnp.bfloat16),
+                ],
+                1,
+            )
+            summed = mxu(left, norm)
+            cos_row = summed[q : q + 1]
+            sin_row = summed[patch_count + q : patch_count + q + 1]
+            cos_b = picked[patch_count + q : patch_count + q + 1, :size]
+            sin_b = picked[patch_count + q : patch_count + q + 1, size:]
+            terms = (cos_row[:, :size] - sin_row[:, size:]) * cos_b - (
+                sin_row[:, :size] + cos_row[:, size:]
+            ) * sin_b
+            score = jnp.sum(terms, axis=1, keepdims=True) * (1.0 / size)
+            score = jnp.broadcast_to(score, (8, size))
+            score_rows = jnp.where(block_row == k * patch_count + q, score, score_rows)
+            weight = 1.0 + 0.5 * jnp.tanh(0.5 * score)
+            column = jnp.full((8, size), info_ref[assign_at + q], jnp.int32)
+            hit = block_row == col * cols + column
+            blocks[plane] = jnp.where(hit, weight, blocks[plane])
+        for plane in range(plane_dev):
+            w_src[k, plane] = blocks[plane]
+        around(lambda j: w_copy(k, j, me).start())
+        w_buf[k, me] = w_src[k, my_plane]
+        if k == 0:
+            around(lambda j: reg_copy(j, j).wait_recv())
+        around(lambda j: w_copy(k, j, j).wait_recv())
+
+        sums = [temp[c, my_plane, my_rows, :].astype(jnp.float32) for c in range(cols)]
+        totals = jnp.ones((8, size), jnp.float32)
+        for v in range(n_tm):
+            weights = w_buf[k, v]
+            totals = totals + weights
+            for c2 in range(cols):
+                piece = reg_buf[v, c2].astype(jnp.float32)
+                for c in range(cols):
+                    row = c2 * cols + c
+                    sums[c] = sums[c] + piece * weights[row : row + 1]
+        for c in range(cols):
+            total = totals[c : c + 1]
+            for c2 in range(1, cols):
+                total = total + (totals[c2 * cols + c : c2 * cols + c + 1] - 1.0)
+            fresh = (sums[c] / total).astype(jnp.bfloat16)
+            if k < ROUNDS - 1:
+                temp_b[c, my_plane, my_rows, :] = fresh
+            else:
+                fin[c] = fresh
+        if k < ROUNDS - 1:
+            around(lambda j: t_copy(j, me).start())
+            around(lambda j: t_copy(j, j).wait_recv())
+
+    everyone(lambda d, j, h: f_copy(d, j, h, flat, me, group).start())
+    out_ref[group * plane_dev + my_plane, my_rows, :] = fin[group]
+    scores_ref[...] = score_rows
+    across(lambda h: swap_copy(h, group).wait_send())
+    around(lambda j: reg_copy(j, me).wait_send())
+    for k in range(ROUNDS):
+        around(lambda j: w_copy(k, j, me).wait_send())
+    around(lambda j: t_copy(j, me).wait_send())
+    everyone(lambda d, j, h: f_copy(d, j, h, d, j, h).wait_recv())
+    everyone(lambda d, j, h: f_copy(d, j, h, flat, me, group).wait_send())
+
+
+def fused(n_tm, cols, frames, offsets, assign, residual, template):
+    plane_dev = frames.shape[1]
+    size = template.shape[2]
+    patch_count = plane_dev * cols
+    info = jnp.concatenate([offsets.reshape(-1), assign.reshape(-1), residual.reshape(-1)])
+    vmem = pl.BlockSpec(memory_space=pltpu.VMEM)
+    dma = pltpu.SemaphoreType.DMA
+    out, scores = pl.pallas_call(
+        functools.partial(fused_kernel, n_tm, cols, plane_dev),
+        out_shape=(
+            jax.ShapeDtypeStruct(template.shape, jnp.bfloat16),
+            jax.ShapeDtypeStruct((8, size), jnp.float32),
+        ),
+        in_specs=[pl.BlockSpec(memory_space=pltpu.SMEM), vmem, vmem, vmem],
+        out_specs=(vmem, vmem),
+        scratch_shapes=[
+            pltpu.VMEM((cols, plane_dev, size, size), jnp.bfloat16),
+            pltpu.VMEM((cols, plane_dev, size, size), jnp.bfloat16),
+            pltpu.VMEM((plane_dev, cols, size, size), jnp.bfloat16),
+            pltpu.VMEM((n_tm, cols, CHUNK, size), jnp.bfloat16),
+            pltpu.VMEM((ROUNDS, plane_dev, 8, size), jnp.float32),
+            pltpu.VMEM((ROUNDS, n_tm, 8, size), jnp.float32),
+            pltpu.VMEM((cols, CHUNK, size), jnp.bfloat16),
+            pltpu.VMEM((patch_count, size, 2 * size), jnp.float32),
+            dma((cols,)),
+            dma((cols,)),
+            dma((n_tm,)),
+            dma((n_tm,)),
+            dma((ROUNDS, n_tm)),
+            dma((ROUNDS, n_tm)),
+            dma((n_tm,)),
+            dma((n_tm,)),
+            dma((n_tm * cols,)),
+            dma((n_tm * cols,)),
+        ],
+        compiler_params=pltpu.CompilerParams(
+            collective_id=0, has_side_effects=True, vmem_limit_bytes=16 * 1024 * 1024
+        ),
+    )(info, frames, template, jnp.asarray(trig_table(size)))
+    scores = scores[: ROUNDS * patch_count, 0].reshape(ROUNDS, 1, plane_dev, 1, cols)
+    return out, scores
+
+
+def dispatch(n_tm, cols, frames, offsets, assign, residual, template):
+    size = template.shape[2]
+    plane_dev = frames.shape[1]
+    width = frames.shape[3]
+    fits = (
+        plane_dev * size == n_tm * CHUNK
+        and template.shape[1] == size
+        and cols * cols <= 8
+        and ROUNDS * plane_dev * cols <= 8
+        and size & (size - 1) == 0
+        and width & (width - 1) == 0
+        and size % 128 == 0
+    )
+    if fits:
+        return fused(n_tm, cols, frames, offsets, assign, residual, template)
+    return local(frames, offsets, assign, residual, template)
+
+
 def solution(mesh):
     return jax.shard_map(
-        local,
+        functools.partial(dispatch, mesh.shape["tm"], mesh.shape["plane"]),
         mesh=mesh,
         in_specs=(
             P("tm", "plane", None, None),

time: 240 us -> 40.5 us (0.17)
  waiting for transfers between devices: 103 us -> 0 us
  blocking collectives: 71.1 us -> 0 us
  Pallas kernels: 0 us -> 33.2 us
  between operations: 14.5 us -> 0.65 us
  local copies, waits for them, and re-layouts: 18.3 us -> 5.69 us
  matrix products: 11.9 us -> 0 us
  starting transfers between devices: 11.1 us -> 0 us
  other arithmetic: 9.81 us -> 0.75 us
    psum x2 -> x0, waiting for transfers between devices: 97.5 us -> none  [renew(): totals, weight_all = lax.psum((tile_sums, weight_sums), 'tm')]
    psum x2 -> x0, blocking collectives: 64.9 us -> none  [renew(): totals, weight_all = lax.psum((tile_sums, weight_sums), 'tm')]
    pallas_call x0 -> x1, Pallas kernels: none -> 33.2 us  [fused(): pl.pallas_call(functools.partial(fused_kernel, n_tm, cols, plane_dev), ou...]
    dot_general x31 -> x0, matrix products: 11.9 us -> none  [the longest x3 2.3 us: spectrum(): jnp.einsum('nyx,xk->nyk', tile_batch, sin_t, preferred_element_type=jnp.f...]
    all_to_all x3 -> x0, starting transfers between devices: 10.8 us -> none  [the longest x1 4.21 us: local(): lax.all_to_all(outgoing_info, 'plane', split_axis=0, concat_axis=0, tiled...]
    gather x12 -> x0, local copies, waits for them, and re-layouts: 9.05 us -> none  [the longest x4 4.46 us: cyclic(): lax.dynamic_slice_in_dim(doubled, (amount % length).astype(jnp.int32), le...]
    all_to_all x1 -> x0, blocking collectives: 6.25 us -> none  [local(): lax.all_to_all(scores, 'plane', split_axis=0, concat_axis=0, tiled=True)]
    all_to_all x3 -> x0, waiting for transfers between devices: 5.04 us -> none  [the longest x1 3.54 us: local(): lax.all_to_all(scores, 'plane', split_axis=0, concat_axis=0, tiled=True)]
  transfers between devices with their start and end apart: 5 -> 0, of which waited for: 4 -> 0; matrix products, arithmetic and copies ran while one was open for 7% -> 0% of each run, Pallas kernels for 0% -> 0%
where the time goes in v1:
time: 40.5 us; the launch traced here: 40.3 us
  Pallas kernels  33.2 us (82%)
  local copies, waits for them, and re-layouts  5.69 us (14%)
  other arithmetic  0.75 us (2%)
  between operations  0.65 us (2%)
    pallas_call x1, Pallas kernels, fused(): pl.pallas_call(functools.partial(fused_kernel, n_tm, cols, plane_dev), ou...  33.2 us
    unnamed x12, local copies, waits for them, and re-layouts  3.99 us

profile of v1, /device:TPU:0, one launch (start us, length us, event | category | flops | bytes accessed | tf_op | source)
XLA Modules:
  0.0 40.3 jit_solution(10077469276521881358)
XLA Ops:
  0.6 0.8 %reshape.13 = s32[4]{0:T(128)S(1)} reshape(s32[1,2,2]{2,1,0:T(2,128)} %param.7) | data formatting | bytes 32 | tf_op jit(solution)/shard_map/reshape | solution.py:468
  1.4 0.0 copy-start.4
  1.4 0.5 %broadcast.4 = s32[]{:T(128)} broadcast(s32[]{:T(128)} %constant.14), dimensions={} | broadcast | bytes 8 | tf_op args[2]
  1.9 0.2 copy-done.4
  2.1 0.0 copy-start.3
  2.1 0.7 %reduce.5 = s32[2,2]{1,0:T(2,128)S(1)} reduce(s32[1,2,1,2,1]{3,4,2,1,0:T(1,128)S(1)} %copy-done.4, s32[]{:T(128)} %broadcast.4), dimensions={0,2,4}, to_apply=%param.8.reduce_sub_computation.3 | reduce | bytes 36 | tf_op args[2]
  2.8 0.1 reshape.14
  2.8 0.0 copy-done.3
  2.8 0.1 reshape.15
  2.9 0.1 pad_add_fusion.info_ref
  3.0 0.0 copy-start
  3.0 0.9 %copy-done = bf16[1,2,128,256]{3,2,1,0:T(8,128)(2,1)S(1)} copy-done((bf16[1,2,128,256]{3,2,1,0:T(8,128)(2,1)S(1)}, bf16[1,2,128,256]{3,2,1,0:T(8,128)(2,1)}, u32[]{:S(2)}) %copy-start) | copy-done | bytes 131096
  3.9 0.0 copy-start.1
  3.9 0.9 %copy-done.1 = bf16[4,128,128]{2,1,0:T(8,128)(2,1)S(1)} copy-done((bf16[4,128,128]{2,1,0:T(8,128)(2,1)S(1)}, bf16[4,128,128]{2,1,0:T(8,128)(2,1)}, u32[]{:S(2)}) %copy-start.1) | copy-done | bytes 131096
  4.8 0.0 copy-start.2
  4.8 0.8 %copy-done.2 = bf16[128,256]{1,0:T(8,128)(2,1)S(1)} copy-done((bf16[128,256]{1,0:T(8,128)(2,1)S(1)}, bf16[128,256]{1,0:T(8,128)(2,1)}, u32[]{:S(2)}) %copy-start.2) | copy-done | bytes 65560
  5.7 33.2 %shard_map.77 = (bf16[4,128,128]{2,1,0:T(8,128)(2,1)S(1)}, f32[8,128]{1,0:T(8,128)S(1)}) custom-call(s32[16]{0:T(128)S(1)} %pad_add_fusion.info_ref, bf16[1,2,128,256]{3,2,1,0:T(8,128)(2,1)S(1)} %copy-done, bf16[4,128,128]{2,1,0:T(8,128)(2,1)S(1)} %copy-done.1, bf16[128,256]{1,0:T(8,128)(2,1)S(1)} %copy-done.2), custom_call_target="tpu_custom_call" | custom-call | tf_op jit(solution)/shard_map/pallas_call | solution.py:471
  38.8 0.1 slice_reduce_fusion
  39.0 0.7 %reshape_squeeze.3 = f32[2,1,2,1,2]{4,2,0,3,1:T(2,128)} reshape(f32[8]{0:T(128)S(1)} %slice_reduce_fusion) | data formatting | bytes 64 | tf_op jit(solution)/shard_map/reshape;squeeze | solution.py:503
  39.6 0.7 %copy.11 = bf16[4,128,128]{2,1,0:T(8,128)(2,1)} copy(bf16[4,128,128]{2,1,0:T(8,128)(2,1)S(1)} %get-tuple-element.12) | data formatting | bytes 262144
Async XLA Ops:
  1.4 0.7 %copy-start.4 = (s32[1,2,1,2,1]{3,4,2,1,0:T(1,128)S(1)}, s32[1,2,1,2,1]{3,4,2,1,0:T(1,128)}, u32[]{:S(2)}) copy-start(s32[1,2,1,2,1]{3,4,2,1,0:T(1,128)} %param.8) | copy-start | bytes 52
  2.1 0.8 %copy-start.3 = (s32[1,2,1,2,2]{4,3,2,1,0:T(2,128)S(1)}, s32[1,2,1,2,2]{4,3,2,1,0:T(2,128)}, u32[]{:S(2)}) copy-start(s32[1,2,1,2,2]{4,3,2,1,0:T(2,128)} %param.9) | copy-start | bytes 100
  3.0 0.9 %copy-start = (bf16[1,2,128,256]{3,2,1,0:T(8,128)(2,1)S(1)}, bf16[1,2,128,256]{3,2,1,0:T(8,128)(2,1)}, u32[]{:S(2)}) copy-start(bf16[1,2,128,256]{3,2,1,0:T(8,128)(2,1)} %frames_ref.1) | copy-start | bytes 393220
  3.9 0.9 %copy-start.1 = (bf16[4,128,128]{2,1,0:T(8,128)(2,1)S(1)}, bf16[4,128,128]{2,1,0:T(8,128)(2,1)}, u32[]{:S(2)}) copy-start(bf16[4,128,128]{2,1,0:T(8,128)(2,1)} %template_ref.1) | copy-start | bytes 393220
  4.8 0.8 %copy-start.2 = (bf16[128,256]{1,0:T(8,128)(2,1)S(1)}, bf16[128,256]{1,0:T(8,128)(2,1)}, u32[]{:S(2)}) copy-start(bf16[128,256]{1,0:T(8,128)(2,1)} %constant.2.clone.table_ref) | copy-start | bytes 196612

commit v2 on v1

--- a/solution.py
+++ b/solution.py
@@ -199,7 +199,8 @@
     return (current, jnp.stack(score_list)[:, None])
 
 
-CHUNK = 16
+REPLICAS = 2
+CHUNK = 16 * REPLICAS
 MESH = pl.DeviceIdType.MESH
 
 
@@ -236,8 +237,8 @@
 
 
 def fused_kernel(
-    n_tm, cols, plane_dev, info_ref, frames_ref, template_ref, table_ref, out_ref, scores_ref,
-    temp_a, temp_b, reg_src, reg_buf, w_src, w_buf, fin, spec,
+    n_tm, cols, plane_dev, offsets_ref, assign_ref, residual_ref, frames_hbm, template_ref, table_hbm,
+    out_ref, scores_ref, frames_ref, table_ref, load_s, temp_a, temp_b, reg_src, reg_buf, w_src, w_buf, fin, spec,
     swap_s, swap_r, reg_s, reg_r, w_s, w_r, t_s, t_r, f_s, f_r,
 ):
     size = table_ref.shape[0]
@@ -245,12 +246,18 @@
     patch_count = plane_dev * cols
     me = lax.axis_index("tm")
     group = lax.axis_index("plane")
-    flat = me * cols + group
-    off_at, assign_at, res_at = 0, 2 * plane_dev, 2 * plane_dev + patch_count
+    units = n_tm // REPLICAS
+    unit = lax.rem(me, units)
+    base = me - unit
+    flat = unit * cols + group
+    assigned = [assign_ref[q // cols, 0, q % cols] for q in range(patch_count)]
+    down = [residual_ref[q // cols, q % cols, 0] for q in range(patch_count)]
+    across_by = [residual_ref[q // cols, q % cols, 1] for q in range(patch_count)]
 
     def place(owner):
-        plane = owner // chunks
-        row = pl.multiple_of((owner % chunks) * CHUNK, CHUNK)
+        owner = lax.rem(owner, units)
+        plane = lax.div(owner, chunks)
+        row = pl.multiple_of(lax.rem(owner, chunks) * CHUNK, CHUNK)
         return plane, pl.ds(row, CHUNK)
 
     my_plane, my_rows = place(me)
@@ -262,6 +269,23 @@
 
         lax.fori_loop(1, n_tm, step, 0)
 
+    def replica(body):
+        def step(r, carry):
+            body(lax.rem(unit + r, units))
+            return carry
+
+        lax.fori_loop(1, units, step, 0)
+
+    def owners_of(plane, first, count, body):
+        def step(r, carry):
+            owner = plane * chunks + lax.rem(unit + r, chunks)
+            for part in range(count):
+                device = first + part * units + owner
+                pl.when(device != me)(functools.partial(body, device))
+            return carry
+
+        lax.fori_loop(0, chunks, step, 0)
+
     def across(body):
         def step(r, carry):
             body(lax.rem(group + r, cols))
@@ -271,11 +295,20 @@
 
     def everyone(body):
         def step(r, carry):
-            other = lax.rem(flat + r, n_tm * cols)
-            body(other, other // cols, lax.rem(other, cols))
+            other = lax.rem(flat + r, units * cols)
+            body(other, lax.div(other, cols), lax.rem(other, cols))
             return carry
 
-        lax.fori_loop(1, n_tm * cols, step, 0)
+        lax.fori_loop(1, units * cols, step, 0)
+
+    frames_load = pltpu.make_async_copy(frames_hbm.at[0], frames_ref, load_s.at[0])
+    table_load = pltpu.make_async_copy(table_hbm, table_ref, load_s.at[1])
+    own_load = pltpu.make_async_copy(
+        template_ref.at[pl.ds(group * plane_dev, plane_dev)], temp_a.at[group], load_s.at[2]
+    )
+    frames_load.start()
+    table_load.start()
+    own_load.start()
 
     barrier = pltpu.get_barrier_semaphore()
     around(
@@ -283,22 +316,17 @@
     )
     across(lambda h: pl.semaphore_signal(barrier, inc=1, device_id=(me, h), device_id_type=MESH))
 
-    table = table_ref[...]
+    frames_load.wait()
 
     patches = []
     for plane in range(plane_dev):
-        frame = frames_ref[0, plane]
-        rows = mxu(wrapped_eye(size, info_ref[off_at + 2 * plane], 0), frame).astype(jnp.bfloat16)
+        frame = frames_ref[plane]
+        rows = mxu(wrapped_eye(size, offsets_ref[plane, 0], 0), frame).astype(jnp.bfloat16)
         shifted = mxu(
-            rows, wrapped_eye(frame.shape[1], info_ref[off_at + 2 * plane + 1], 1)
+            rows, wrapped_eye(frame.shape[1], offsets_ref[plane, 1], 1)
         ).astype(jnp.bfloat16)
         for col in range(cols):
             patches.append(shifted[:, col * size : (col + 1) * size])
-    for q, patch in enumerate(patches):
-        rolled = mxu(wrapped_eye(size, info_ref[res_at + 2 * q], 0), patch).astype(jnp.bfloat16)
-        rolled = mxu(rolled, wrapped_eye(size, info_ref[res_at + 2 * q + 1], 1))
-        reg_src[q // cols, q % cols] = rolled.astype(jnp.bfloat16)
-
     pl.semaphore_wait(barrier, n_tm - 1 + cols - 1)
 
     def swap_copy(to, slot):
@@ -324,7 +352,7 @@
 
     def w_copy(k, to, slot):
         return pltpu.make_async_remote_copy(
-            src_ref=w_src.at[k, to // chunks],
+            src_ref=w_src.at[k, lax.div(lax.rem(to, units), chunks)],
             dst_ref=w_buf.at[k, slot],
             send_sem=w_s.at[k, to],
             recv_sem=w_r.at[k, slot],
@@ -339,7 +367,7 @@
             dst_ref=temp_b.at[:, plane, rows, :],
             send_sem=t_s.at[to],
             recv_sem=t_r.at[owner],
-            device_id=(to, group),
+            device_id=(base + to, group),
             device_id_type=MESH,
         )
 
@@ -350,15 +378,19 @@
             dst_ref=out_ref.at[owner_plane * plane_dev + plane, rows, :],
             send_sem=f_s.at[to],
             recv_sem=f_r.at[owner],
-            device_id=(to_tm, to_plane),
+            device_id=(base + to_tm, to_plane),
             device_id_type=MESH,
         )
 
     across(lambda h: swap_copy(h, group).start())
+    table_load.wait()
+    table = table_ref[...].astype(jnp.bfloat16)
+    for q, patch in enumerate(patches):
+        rolled = mxu(wrapped_eye(size, down[q], 0), patch).astype(jnp.bfloat16)
+        rolled = mxu(rolled, wrapped_eye(size, across_by[q], 1))
+        reg_src[q // cols, q % cols] = rolled.astype(jnp.bfloat16)
     around(lambda j: reg_copy(j, me).start())
-    temp_a[group] = template_ref[pl.ds(group * plane_dev, plane_dev)]
     reg_buf[me] = reg_src[my_plane, :, my_rows, :]
-
     for q, patch in enumerate(patches):
         spec[q] = two_stage(patch, table)
 
@@ -366,24 +398,28 @@
     lane_id = lax.broadcasted_iota(jnp.int32, (2 * patch_count, size), 1)
     wanted = jnp.zeros((2 * patch_count, size), jnp.int32)
     for q in range(patch_count):
-        wanted = jnp.where(row_id == q, info_ref[res_at + 2 * q], wanted)
-        wanted = jnp.where(row_id == patch_count + q, info_ref[res_at + 2 * q + 1], wanted)
+        wanted = jnp.where(row_id == q, down[q], wanted)
+        wanted = jnp.where(row_id == patch_count + q, across_by[q], wanted)
     onehot = ((wanted & (size - 1)) == lane_id).astype(jnp.float32).astype(jnp.bfloat16)
     picked = mxu(onehot, table)
     left = jnp.concatenate(
         [picked[:patch_count, :size], picked[:patch_count, size:]], 0
     ).astype(jnp.bfloat16)
 
-    block_row = lax.broadcasted_iota(jnp.int32, (8, size), 0)
+    own_load.wait()
     across(lambda h: swap_copy(h, h).wait_recv())
 
-    score_rows = jnp.zeros((8, size), jnp.float32)
+    lane_at = lax.broadcasted_iota(jnp.int32, (1, size), 1)
     for k in range(ROUNDS):
         temp = temp_a if k == 0 else temp_b
-        blocks = [jnp.zeros((8, size), jnp.float32) for _ in range(plane_dev)]
         for q in range(patch_count):
             plane, col = q // cols, q % cols
-            target = jnp.full((size, size), info_ref[assign_at + q], jnp.int32)
+            if col == 0:
+                score_row = jnp.zeros((1, size), jnp.float32)
+                weight_row = jnp.zeros((1, size), jnp.float32)
+                if k > 0:
+                    owners_of(plane, base, 1, lambda j: t_copy(j - base, j - base).wait_recv())
+            target = jnp.full((size, size), assigned[q], jnp.int32)
             tile = temp[0, plane].astype(jnp.float32)
             for c in range(1, cols):
                 tile = jnp.where(target == c, temp[c, plane].astype(jnp.float32), tile)
@@ -412,77 +448,89 @@
                 sin_row[:, :size] + cos_row[:, size:]
             ) * sin_b
             score = jnp.sum(terms, axis=1, keepdims=True) * (1.0 / size)
-            score = jnp.broadcast_to(score, (8, size))
-            score_rows = jnp.where(block_row == k * patch_count + q, score, score_rows)
+            score = jnp.broadcast_to(score, (8, size))[:1]
+            score_row = jnp.where(lane_at == col, score, score_row)
             weight = 1.0 + 0.5 * jnp.tanh(0.5 * score)
-            column = jnp.full((8, size), info_ref[assign_at + q], jnp.int32)
-            hit = block_row == col * cols + column
-            blocks[plane] = jnp.where(hit, weight, blocks[plane])
-        for plane in range(plane_dev):
-            w_src[k, plane] = blocks[plane]
-        around(lambda j: w_copy(k, j, me).start())
+            target_row = jnp.full((1, size), assigned[q], jnp.int32)
+            weight_row = jnp.where(lane_at == col * cols + target_row, weight, weight_row)
+            if col == cols - 1:
+                w_src[k, plane] = weight_row
+                owners_of(plane, 0, REPLICAS, lambda j: w_copy(k, j, me).start())
+                scores_ref[k, 0, plane] = score_row[:, :cols]
         w_buf[k, me] = w_src[k, my_plane]
         if k == 0:
             around(lambda j: reg_copy(j, j).wait_recv())
         around(lambda j: w_copy(k, j, j).wait_recv())
 
         sums = [temp[c, my_plane, my_rows, :].astype(jnp.float32) for c in range(cols)]
-        totals = jnp.ones((8, size), jnp.float32)
+        lanes = lax.broadcasted_iota(jnp.int32, (n_tm, size), 1)
+        gathered = w_buf[k].reshape(n_tm, size)
+        spread = [
+            jnp.broadcast_to(
+                jnp.sum(jnp.where(lanes == row, gathered, 0.0), axis=1, keepdims=True),
+                (n_tm, size),
+            )
+            for row in range(cols * cols)
+        ]
         for v in range(n_tm):
-            weights = w_buf[k, v]
-            totals = totals + weights
             for c2 in range(cols):
                 piece = reg_buf[v, c2].astype(jnp.float32)
                 for c in range(cols):
-                    row = c2 * cols + c
-                    sums[c] = sums[c] + piece * weights[row : row + 1]
+                    sums[c] = sums[c] + piece * spread[c2 * cols + c][v : v + 1]
         for c in range(cols):
-            total = totals[c : c + 1]
+            weights = spread[c]
             for c2 in range(1, cols):
-                total = total + (totals[c2 * cols + c : c2 * cols + c + 1] - 1.0)
+                weights = weights + spread[c2 * cols + c]
+            total = 1.0 + jnp.sum(weights, axis=0, keepdims=True)
             fresh = (sums[c] / total).astype(jnp.bfloat16)
             if k < ROUNDS - 1:
                 temp_b[c, my_plane, my_rows, :] = fresh
             else:
                 fin[c] = fresh
         if k < ROUNDS - 1:
-            around(lambda j: t_copy(j, me).start())
-            around(lambda j: t_copy(j, j).wait_recv())
-
-    everyone(lambda d, j, h: f_copy(d, j, h, flat, me, group).start())
-    out_ref[group * plane_dev + my_plane, my_rows, :] = fin[group]
-    scores_ref[...] = score_rows
+            replica(lambda u: t_copy(u, unit).start())
+
+    everyone(lambda d, j, h: f_copy(d, j, h, flat, unit, group).start())
+    own_store = pltpu.make_async_copy(
+        fin.at[group], out_ref.at[group * plane_dev + my_plane, my_rows, :], load_s.at[3]
+    )
+    own_store.start()
     across(lambda h: swap_copy(h, group).wait_send())
     around(lambda j: reg_copy(j, me).wait_send())
     for k in range(ROUNDS):
         around(lambda j: w_copy(k, j, me).wait_send())
-    around(lambda j: t_copy(j, me).wait_send())
+    replica(lambda u: t_copy(u, unit).wait_send())
+    own_store.wait()
     everyone(lambda d, j, h: f_copy(d, j, h, d, j, h).wait_recv())
-    everyone(lambda d, j, h: f_copy(d, j, h, flat, me, group).wait_send())
+    everyone(lambda d, j, h: f_copy(d, j, h, flat, unit, group).wait_send())
 
 
 def fused(n_tm, cols, frames, offsets, assign, residual, template):
     plane_dev = frames.shape[1]
     size = template.shape[2]
     patch_count = plane_dev * cols
-    info = jnp.concatenate([offsets.reshape(-1), assign.reshape(-1), residual.reshape(-1)])
     vmem = pl.BlockSpec(memory_space=pltpu.VMEM)
+    smem = pl.BlockSpec(memory_space=pltpu.SMEM)
+    hbm = pl.BlockSpec(memory_space=pltpu.HBM)
     dma = pltpu.SemaphoreType.DMA
-    out, scores = pl.pallas_call(
+    return pl.pallas_call(
         functools.partial(fused_kernel, n_tm, cols, plane_dev),
         out_shape=(
             jax.ShapeDtypeStruct(template.shape, jnp.bfloat16),
-            jax.ShapeDtypeStruct((8, size), jnp.float32),
+            jax.ShapeDtypeStruct((ROUNDS, 1, plane_dev, 1, cols), jnp.float32),
         ),
-        in_specs=[pl.BlockSpec(memory_space=pltpu.SMEM), vmem, vmem, vmem],
-        out_specs=(vmem, vmem),
+        in_specs=[smem, smem, smem, hbm, hbm, hbm],
+        out_specs=(hbm, vmem),
         scratch_shapes=[
+            pltpu.VMEM(frames.shape[1:], jnp.bfloat16),
+            pltpu.VMEM((size, 2 * size), jnp.float32),
+            dma((4,)),
             pltpu.VMEM((cols, plane_dev, size, size), jnp.bfloat16),
             pltpu.VMEM((cols, plane_dev, size, size), jnp.bfloat16),
             pltpu.VMEM((plane_dev, cols, size, size), jnp.bfloat16),
             pltpu.VMEM((n_tm, cols, CHUNK, size), jnp.bfloat16),
-            pltpu.VMEM((ROUNDS, plane_dev, 8, size), jnp.float32),
-            pltpu.VMEM((ROUNDS, n_tm, 8, size), jnp.float32),
+            pltpu.VMEM((ROUNDS, plane_dev, 1, size), jnp.float32),
+            pltpu.VMEM((ROUNDS, n_tm, 1, size), jnp.float32),
             pltpu.VMEM((cols, CHUNK, size), jnp.bfloat16),
             pltpu.VMEM((patch_count, size, 2 * size), jnp.float32),
             dma((cols,)),
@@ -491,17 +539,22 @@
             dma((n_tm,)),
             dma((ROUNDS, n_tm)),
             dma((ROUNDS, n_tm)),
-            dma((n_tm,)),
-            dma((n_tm,)),
-            dma((n_tm * cols,)),
-            dma((n_tm * cols,)),
+            dma((n_tm // REPLICAS,)),
+            dma((n_tm // REPLICAS,)),
+            dma((n_tm // REPLICAS * cols,)),
+            dma((n_tm // REPLICAS * cols,)),
         ],
         compiler_params=pltpu.CompilerParams(
-            collective_id=0, has_side_effects=True, vmem_limit_bytes=16 * 1024 * 1024
+            collective_id=0, has_side_effects=True
         ),
-    )(info, frames, template, jnp.asarray(trig_table(size)))
-    scores = scores[: ROUNDS * patch_count, 0].reshape(ROUNDS, 1, plane_dev, 1, cols)
-    return out, scores
+    )(
+        offsets.reshape(plane_dev, 2),
+        assign.reshape(plane_dev, 1, cols),
+        residual.reshape(plane_dev, cols, 2),
+        frames,
+        template,
+        jnp.asarray(trig_table(size).astype(np.float32)),
+    )
 
 
 def dispatch(n_tm, cols, frames, offsets, assign, residual, template):
@@ -509,10 +562,11 @@
     plane_dev = frames.shape[1]
     width = frames.shape[3]
     fits = (
-        plane_dev * size == n_tm * CHUNK
+        n_tm % REPLICAS == 0
+        and plane_dev * size == n_tm // REPLICAS * CHUNK
         and template.shape[1] == size
         and cols * cols <= 8
-        and ROUNDS * plane_dev * cols <= 8
+        and 2 * plane_dev * cols <= 8
         and size & (size - 1) == 0
         and width & (width - 1) == 0
         and size % 128 == 0

time: 40.5 us -> 33.2 us (0.82)
  local copies, waits for them, and re-layouts: 5.69 us -> 2.15 us
  Pallas kernels: 33.2 us -> 30.2 us
  other arithmetic: 0.75 us -> 0 us
    pallas_call x1, Pallas kernels: 33.2 us -> 30.2 us  [fused(): pl.pallas_call(functools.partial(fused_kernel, n_tm, cols, plane_dev), ou...]
    unnamed x12 -> x4, local copies, waits for them, and re-layouts: 3.99 us -> 2.15 us
    reshape x3 -> x0, local copies, waits for them, and re-layouts: 0.93 us -> none  [the longest x1 0.76 us: fused(): offsets.reshape(-1)]
    unnamed x1 -> x0, other arithmetic: 0.68 us -> none
    another operation x1 -> x0, local copies, waits for them, and re-layouts: 0.67 us -> none  [fused(): scores[:ROUNDS * patch_count, 0].reshape(ROUNDS, 1, plane_dev, 1, cols)]
where the time goes in v2:
time: 33.2 us; the launch traced here: 33 us
  Pallas kernels  30.2 us (91%)
  local copies, waits for them, and re-layouts  2.15 us (6%)
  between operations  0.65 us (2%)
    pallas_call x1, Pallas kernels, fused(): pl.pallas_call(functools.partial(fused_kernel, n_tm, cols, plane_dev), ou...  30.2 us
    unnamed x4, local copies, waits for them, and re-layouts  2.15 us

profile of v2, /device:TPU:0, one launch (start us, length us, event | category | flops | bytes accessed | tf_op | source)
XLA Modules:
  0.0 33.0 jit_solution(3164543322052792246)
XLA Ops:
  0.6 30.2 %shard_map.77 = (bf16[4,128,128]{2,1,0:T(8,128)(2,1)}, f32[2,1,2,1,2]{4,3,2,1,0:T(1,128)}) custom-call(s32[2,2]{1,0:T(2,128)} %bitcast.6, s32[2,1,2]{2,1,0:T(1,128)} %bitcast.7, s32[2,2,2]{2,1,0:T(2,128)} %bitcast.5, bf16[1,2,128,256]{3,2,1,0:T(8,128)(2,1)} %frames_hbm.1, bf16[4,128,128]{2,1,0:T(8,128)(2,1)} %template_ref.1, f32[128,256]{1,0:T(8,128)} %constant.2.clone.table_hbm), custom_call_target="tpu_custom_call" | custom-call | tf_op jit(solution)/shard_map/pallas_call | solution.py:516
  30.8 0.0 copy-start
  30.8 1.6 %copy.11 = bf16[4,128,128]{2,1,0:T(8,128)(2,1)} copy(bf16[4,128,128]{2,1,0:T(8,128)(2,1)} %get-tuple-element.4) | data formatting | bytes 262144
  32.4 0.0 copy-done
  32.4 0.6 %copy.12 = f32[2,1,2,1,2]{4,3,2,1,0:T(1,128)} copy(f32[2,1,2,1,2]{4,3,2,1,0:T(1,128)S(1)} %copy-done) | data formatting | bytes 64
Async XLA Ops:
  30.8 1.6 %copy-start = (f32[2,1,2,1,2]{4,3,2,1,0:T(1,128)S(1)}, f32[2,1,2,1,2]{4,3,2,1,0:T(1,128)}, u32[]{:S(2)}) copy-start(f32[2,1,2,1,2]{4,3,2,1,0:T(1,128)} %get-tuple-element.5) | copy-start | bytes 100

commit v3 on v2

--- a/solution.py
+++ b/solution.py
@@ -327,6 +327,11 @@
         ).astype(jnp.bfloat16)
         for col in range(cols):
             patches.append(shifted[:, col * size : (col + 1) * size])
+    for q, patch in enumerate(patches):
+        rolled = mxu(wrapped_eye(size, down[q], 0), patch).astype(jnp.bfloat16)
+        rolled = mxu(rolled, wrapped_eye(size, across_by[q], 1))
+        reg_src[q // cols, q % cols] = rolled.astype(jnp.bfloat16)
+
     pl.semaphore_wait(barrier, n_tm - 1 + cols - 1)
 
     def swap_copy(to, slot):
@@ -383,14 +388,10 @@
         )
 
     across(lambda h: swap_copy(h, group).start())
+    around(lambda j: reg_copy(j, me).start())
+    reg_buf[me] = reg_src[my_plane, :, my_rows, :]
     table_load.wait()
     table = table_ref[...].astype(jnp.bfloat16)
-    for q, patch in enumerate(patches):
-        rolled = mxu(wrapped_eye(size, down[q], 0), patch).astype(jnp.bfloat16)
-        rolled = mxu(rolled, wrapped_eye(size, across_by[q], 1))
-        reg_src[q // cols, q % cols] = rolled.astype(jnp.bfloat16)
-    around(lambda j: reg_copy(j, me).start())
-    reg_buf[me] = reg_src[my_plane, :, my_rows, :]
     for q, patch in enumerate(patches):
         spec[q] = two_stage(patch, table)
 
@@ -505,6 +506,51 @@
     everyone(lambda d, j, h: f_copy(d, j, h, flat, unit, group).wait_send())
 
 
+def handing_on_kernel(
+    parts, template_in, scores_in, template_out, scores_out, template_mid, scores_mid, load, store
+):
+    rows = template_in.shape[0] // parts
+    moves = [(scores_in, scores_mid, scores_out)]
+    for part in range(parts):
+        here = pl.ds(part * rows, rows)
+        moves.append((template_in.at[here], template_mid.at[here], template_out.at[here]))
+    loads = [
+        pltpu.make_async_copy(source, middle, load.at[i])
+        for i, (source, middle, _) in enumerate(moves)
+    ]
+    stores = [
+        pltpu.make_async_copy(middle, target, store.at[i])
+        for i, (_, middle, target) in enumerate(moves)
+    ]
+    for copy in loads:
+        copy.start()
+    for arrival, departure in zip(loads, stores):
+        arrival.wait()
+        departure.start()
+    for copy in stores:
+        copy.wait()
+
+
+def handing_on(template, scores):
+    parts = template.shape[0]
+    hbm = pl.BlockSpec(memory_space=pltpu.HBM)
+    return pl.pallas_call(
+        functools.partial(handing_on_kernel, parts),
+        out_shape=(
+            jax.ShapeDtypeStruct(template.shape, template.dtype),
+            jax.ShapeDtypeStruct(scores.shape, scores.dtype),
+        ),
+        in_specs=[hbm, hbm],
+        out_specs=(hbm, hbm),
+        scratch_shapes=[
+            pltpu.VMEM(template.shape, template.dtype),
+            pltpu.VMEM(scores.shape, scores.dtype),
+            pltpu.SemaphoreType.DMA((parts + 1,)),
+            pltpu.SemaphoreType.DMA((parts + 1,)),
+        ],
+    )(template, scores)
+
+
 def fused(n_tm, cols, frames, offsets, assign, residual, template):
     plane_dev = frames.shape[1]
     size = template.shape[2]
@@ -572,7 +618,7 @@
         and size % 128 == 0
     )
     if fits:
-        return fused(n_tm, cols, frames, offsets, assign, residual, template)
+        return handing_on(*fused(n_tm, cols, frames, offsets, assign, residual, template))
     return local(frames, offsets, assign, residual, template)
 
 

time: 33.2 us -> 32.3 us (0.973)
  local copies, waits for them, and re-layouts: 2.15 us -> 0 us
  Pallas kernels: 30.2 us -> 31.4 us
    unnamed x4 -> x0, local copies, waits for them, and re-layouts: 2.15 us -> none
    pallas_call x0 -> x1, Pallas kernels: none -> 1.51 us  [handing_on(): pl.pallas_call(functools.partial(handing_on_kernel, parts), out_shape=(ja...]
where the time goes in v3:
time: 32.3 us; the launch traced here: 32 us
  Pallas kernels  31.4 us (97%)
  between operations  0.64 us (2%)
    pallas_call x1, Pallas kernels, fused(): pl.pallas_call(functools.partial(fused_kernel, n_tm, cols, plane_dev), ou...  29.9 us
    pallas_call x1, Pallas kernels, handing_on(): pl.pallas_call(functools.partial(handing_on_kernel, parts), out_shape=(ja...  1.51 us

profile of v3, /device:TPU:0, one launch (start us, length us, event | category | flops | bytes accessed | tf_op | source)
XLA Modules:
  0.0 32.0 jit_solution(7674811056427587363)
XLA Ops:
  0.6 29.9 %shard_map.77 = (bf16[4,128,128]{2,1,0:T(8,128)(2,1)}, f32[2,1,2,1,2]{4,3,2,1,0:T(1,128)}) custom-call(s32[2,2]{1,0:T(2,128)} %bitcast.6, s32[2,1,2]{2,1,0:T(1,128)} %bitcast.7, s32[2,2,2]{2,1,0:T(2,128)} %bitcast.5, bf16[1,2,128,256]{3,2,1,0:T(8,128)(2,1)} %frames_hbm.1, bf16[4,128,128]{2,1,0:T(8,128)(2,1)} %template_ref.1, f32[128,256]{1,0:T(8,128)} %constant.2.clone.table_hbm), custom_call_target="tpu_custom_call" | custom-call | tf_op jit(solution)/shard_map/pallas_call | solution.py:562
  30.5 1.5 %shard_map.78 = (bf16[4,128,128]{2,1,0:T(8,128)(2,1)}, f32[2,1,2,1,2]{4,3,2,1,0:T(1,128)}) custom-call(bf16[4,128,128]{2,1,0:T(8,128)(2,1)} %get-tuple-element.4.template_in, f32[2,1,2,1,2]{4,3,2,1,0:T(1,128)} %get-tuple-element.5.scores_in), custom_call_target="tpu_custom_call" | custom-call | tf_op jit(solution)/shard_map/pallas_call | solution.py:537
